TPU v7x, 128 devices: a whole 4x4x4 slice. The times are simulated.
128 devices in a mesh: beam: 32 (over z, y, core), sub: 4 (over x).
Axes of the slice: x: 4, y: 4, z: 4, core: 2. Of those that a mesh axis runs over, the one named last changes fastest.
Arguments:
- voltages: bfloat16 [2, 32, 4, 798, 256], P(None, 'beam', 'sub'), may hold values from -6 to 6
- pfb_taps: float32 [16, 256], replicated, may hold values from -1.5 to 1.5
- delays: int32 [2048, 1024], replicated, may hold values from 0 to 15, as said below
- assignment: int32 [32, 32], replicated, may hold values from 0 to 31, each once within a row
- widths: int32 [8], replicated, may hold values from 1 to 32
Outputs:
- dm_series: bfloat16 [32, 32, 64, 768], P('beam', None, 'sub')
- snr: float32 [32, 32, 64, 8], P('beam', None, 'sub')
Inputs may be any that keep to these rules, and one draw needn't show every extreme that they name: delays are nonnegative and below 16. Each row of assignment names every one of the 32 DM ranges once.
All inputs are finite; a program needn't handle non-finite values.
Results may differ from a plain program's by a relative error of at most 0.0048.
Values may be sent and summed in bfloat16 or wider, within the bound.
A program may use at most 128 MiB of HBM per device.

v0:
```python
import math

import jax
import jax.numpy as jnp
from jax import lax
from jax.sharding import PartitionSpec as P

FINE = 256
COARSE = 4
SHIFTS = 16
NBOX = 8
TOUT = 768


HIGHEST = lax.Precision.HIGHEST


def dft_table(fine_len):
    position = jnp.arange(fine_len, dtype=jnp.int32)
    phases = position[:, None] * position[None, :] % fine_len
    angles = phases.astype(jnp.float32) * (2.0 * math.pi / fine_len)
    cosine = jnp.cos(angles) / math.sqrt(fine_len)
    sine_part = jnp.sin(angles) / math.sqrt(fine_len)
    upper_half = jnp.concatenate([cosine, -sine_part], axis=1)
    lower_half = jnp.concatenate([sine_part, cosine], axis=1)
    return jnp.concatenate([upper_half, lower_half], axis=0)


def channelize(voltages, pfb_taps):
    frames = voltages.astype(jnp.float32)
    frames_out = frames.shape[-2] - pfb_taps.shape[0] + 1
    filtered = pfb_taps[0] * frames[..., 0:frames_out, :]
    for tap_index in range(1, pfb_taps.shape[0]):
        filtered = (
            filtered + pfb_taps[tap_index] * frames[..., tap_index : tap_index + frames_out, :]
        )
    fine_len = pfb_taps.shape[1]
    stacked = jnp.concatenate([filtered[0], filtered[1]], axis=-1)
    spectra = jnp.dot(
        stacked, dft_table(fine_len), precision=HIGHEST, preferred_element_type=jnp.float32
    )
    powers = spectra[..., :fine_len] ** 2 + spectra[..., fine_len:] ** 2
    return (powers - jnp.mean(powers, axis=-2, keepdims=True)).astype(jnp.bfloat16)


def boxcar_table(widths, length):
    position = jnp.arange(length, dtype=jnp.int32)
    upper_ids = position[:, None, None]
    lower_ids = position[None, None, :]
    return (upper_ids >= lower_ids) & (upper_ids < lower_ids + widths[None, :, None])


def delay_sum(lookup, power_rows):
    levels = jnp.arange(SHIFTS, dtype=jnp.int32)
    table = (lookup[None, :, :] == levels[:, None, None]).astype(jnp.bfloat16)
    product = jnp.einsum("src,tc->srt", table, power_rows, preferred_element_type=jnp.float32)
    total = product[0, :, 0:TOUT]
    for shift_level in range(1, SHIFTS):
        total = total + product[shift_level, :, shift_level : shift_level + TOUT]
    return total


def on_device(voltages, pfb_taps, delays, assignment, widths):
    fine_power = channelize(voltages, pfb_taps)[0, 0]
    beam_count = lax.axis_size("beam")
    dm_span = delays.shape[0] // beam_count
    my_beam = lax.axis_index("beam")
    my_sub = lax.axis_index("sub")
    norm_scale = (COARSE * FINE) ** (-0.5)
    local_delays = lax.dynamic_slice_in_dim(delays, my_sub * FINE, FINE, 1)
    piece = lax.all_gather(fine_power[None], "beam", axis=0, tiled=True)
    sources = jnp.arange(piece.shape[0], dtype=jnp.int32)

    def one_source(inputs):
        beam_slab, anchor = inputs
        offset = assignment[anchor, my_beam] * dm_span
        lookup = lax.dynamic_slice_in_dim(local_delays, offset, dm_span, 0)
        return delay_sum(lookup, beam_slab)

    partial_value = lax.map(one_source, (piece, sources))
    summed = lax.psum_scatter(partial_value, "sub", scatter_dimension=1, tiled=True)
    dm_series = (summed * norm_scale).astype(jnp.bfloat16)
    flattened = dm_series.reshape(-1, TOUT)
    lookup = boxcar_table(widths, TOUT).astype(jnp.bfloat16).reshape(TOUT, NBOX * TOUT)
    box_sums = jnp.dot(flattened, lookup, preferred_element_type=jnp.float32)
    best = jnp.max(box_sums.reshape(-1, NBOX, TOUT), axis=-1) / jnp.sqrt(widths.astype(jnp.float32))
    snr = best.reshape(1, beam_count, dm_series.shape[1], NBOX)
    return (dm_series[None], snr)


def solution(mesh):
    in_specs = (P(None, "beam", "sub", None, None), P(), P(), P(), P())
    out_specs = (P("beam", None, "sub", None), P("beam", None, "sub", None))
    return jax.shard_map(
        on_device, mesh=mesh, in_specs=in_specs, out_specs=out_specs, check_vma=False
    )
```

profile of v0, /device:TPU:1, one launch (start us, length us, event | category | flops | bytes accessed | tf_op | source)
XLA Modules:
  0.0 423.7 jit_solution(11596955969900102285)
XLA Ops:
  10.3 1.7 convert_element_type.23
  12.0 8.6 %fusion.10 = f32[2,1,1,783,256]{4,0,3,2,1:T(2,128)S(1)} fusion(f32[2,1,1,798,256]{4,0,3,2,1:T(2,128)S(1)} %convert_element_type.23, f32[256]{0:T(256)S(1)} %bitcast.73, f32[256]{0:T(256)S(1)} %bitcast.74, f32[256]{0:T(256)S(1)} %bitcast.60, f32[256]{0:T(256)S(1)} %bitcast.61, f32[256]{0:T(256)S(1)} %bitcast.62, f32[256]{0:T(256)S(1)} %bitcast.63, ...), kind=kLoop, calls=%fused_computation.31 | loop fusion | flops 12427776 | bytes 27277312 | tf_op jit(solution)/shard_map/add | solution.py:35
  23.3 2.7 fusion.25
  27.3 1.7 constant_dynamic-slice_fusion.1
  29.0 65.4 %all-gather.3.cloned.1.call-done = bf16[32,1,783,256]{3,2,1,0:T(8,128)(2,1)} async-done(((bf16[1,1,783,256]{3,2,1,0:T(8,128)(2,1)}), bf16[32,1,783,256]{3,2,1,0:T(8,128)(2,1)}) %all-gather.3.cloned.1.call-update) | async-done | bytes 12828688 | tf_op jit(solution)/shard_map/all_gather | solution.py:71
  94.4 247.9 %while.12 = (s32[]{:T(128)}, f32[32,64,768]{2,1,0:T(8,128)}, s32[32]{0:T(128)S(1)}, s32[32,32]{1,0:T(8,128)}, s32[]{:T(128)}, /*index=5*/s32[2048,256]{1,0:T(8,1...) while((s32[]{:T(128)}, f32[32,64,768]{2,1,0:T(8,128)}, ...), condition=%wide.region_2.3_spmd, body=%wide.region_1.2_spmd.sunk | while | flops 411516928 | bytes 7148769 | solution.py:80
  98.9 1.7 fusion.53
  100.6 1.5 fusion.54
  106.6 1.7 fusion.53
  108.4 1.5 fusion.54
  114.4 1.7 fusion.53
  116.1 1.5 fusion.54
  122.1 1.7 fusion.53
  123.9 1.5 fusion.54
  129.9 1.7 fusion.53
  137.6 1.7 fusion.53
  145.3 1.7 fusion.53
  147.1 1.5 fusion.54
  153.1 1.7 fusion.53
  160.8 1.7 fusion.53
  162.6 1.5 fusion.54
  168.6 1.7 fusion.53
  170.3 1.5 fusion.54
  176.3 1.7 fusion.53
  178.1 1.5 fusion.54
  184.1 1.7 fusion.53
  191.8 1.7 fusion.53
  193.6 1.5 fusion.54
  199.6 1.7 fusion.53
  201.3 1.5 fusion.54
  207.3 1.7 fusion.53
  209.1 1.5 fusion.54
  215.1 1.7 fusion.53
  222.8 1.7 fusion.53
  230.6 1.7 fusion.53
  232.3 1.5 fusion.54
  238.3 1.7 fusion.53
  246.0 1.7 fusion.53
  247.8 1.5 fusion.54
  253.8 1.7 fusion.53
  255.5 1.5 fusion.54
  261.5 1.7 fusion.53
  263.3 1.5 fusion.54
  269.3 1.7 fusion.53
  277.0 1.7 fusion.53
  278.8 1.5 fusion.54
  284.8 1.7 fusion.53
  286.5 1.5 fusion.54
  292.5 1.7 fusion.53
  294.3 1.5 fusion.54
  300.3 1.7 fusion.53
  308.0 1.7 fusion.53
  309.8 1.5 fusion.54
  315.8 1.7 fusion.53
  317.5 1.5 fusion.54
  323.5 1.7 fusion.53
  325.2 1.5 fusion.54
  331.2 1.7 fusion.53
  339.0 1.7 fusion.53
  340.7 1.5 fusion.54
  343.2 7.4 %fusion.6 = pred[768,6144]{0,1:T(32,128)(4,1)} fusion(s32[6144]{0:T(1024)S(1)} %add.220, pred[768,768]{0,1:T(8,128)(4,1)S(1)} %iota_compare_fusion.3), kind=kLoop, calls=%fused_computation.24 | loop fusion | flops 9437184 | bytes 5332992 | tf_op jit(solution)/shard_map/and | solution.py:50
  350.6 54.8 %reduce-scatter.2.cloned.1.call-done = f32[32,16,768]{2,1,0:T(8,128)} async-done(((f32[32,64,768]{2,1,0:T(8,128)}), f32[32,16,768]{2,1,0:T(8,128)}) %reduce-scatter.2.cloned.1.call-update) | async-done | bytes 1572880 | tf_op jit(solution)/shard_map/reduce_scatter | solution.py:81
  405.4 1.5 multiply_convert_fusion
  406.9 8.0 %convolution_reduce_fusion = f32[512,8]{0,1:T(8,128)S(1)} fusion(bf16[512,768,1]{1,0,2:T(8,128)(2,1)S(1)} %bitcast.56, pred[8,768,768]{2,1,0:T(32,128)(4,1)} %bitcast.55), kind=kOutput, calls=%fused_computation.25 | convolution fusion | flops 4834979840 | bytes 5521408 | tf_op jit(solution)/shard_map/dot_general | solution.py:85
  (134 shorter events, 84.7 us)
Async XLA Ops:
  7.2 87.2 %all-gather.3.cloned.1.call-start = ((), (), s32[]{:S(2)}) async-start(), calls=%async_computation.2 | async-start | bytes 13246464 | tf_op jit(solution)/shard_map/all_gather | solution.py:71
  27.0 378.4 %reduce-scatter.2.cloned.1.call-start = ((), (), s32[]{:S(2)}) async-start(), calls=%async_computation.1 | async-start | bytes 7864320 | tf_op jit(solution)/shard_map/reduce_scatter | solution.py:81
  342.2 0.7 copy-start.1
  406.9 9.0 %copy-start = (f32[32,16,768]{2,1,0:T(8,128)S(1)}, f32[32,16,768]{2,1,0:T(8,128)}, u32[]{:S(2)}) copy-start(f32[32,16,768]{2,1,0:T(8,128)} %reduce-scatter.2.cloned.1.call-done) | copy-start | bytes 4718596
Sparse Core Ops, SparseCore 0:
  27.2 67.1 all-gather.2
  342.4 62.9 reduce-scatter.1
where the time goes:
time: 427 us; the launch traced here: 424 us
  waiting for transfers between devices  120 us (28%)
  loops' own time  83.7 us (20%)
  other arithmetic  73.4 us (17%)
  matrix products  66.6 us (16%)
  local copies, waits for them, and re-layouts  65.4 us (15%)
  between operations  14.2 us (3%)
    another operation x1, loops' own time, on_device(): partial_value = lax.map(one_source, (piece, sources))  83.7 us
    all_gather x1, waiting for transfers between devices, on_device(): piece = lax.all_gather(fine_power[None], 'beam', axis=0, tiled=True)  65.4 us
    dot_general x32, matrix products, delay_sum(): jnp.einsum('src,tc->srt', table, power_rows, preferred_element_type=jnp.f...  55.9 us
    reduce_scatter x1, waiting for transfers between devices, on_device(): lax.psum_scatter(partial_value, 'sub', scatter_dimension=1, tiled=True)  54.8 us
    dynamic_update_slice x32, other arithmetic, on_device(): partial_value = lax.map(one_source, (piece, sources))  48.4 us
    dynamic_slice x32, local copies, waits for them, and re-layouts, one_source(): offset = assignment[anchor, my_beam] * dm_span  40.8 us
    dynamic_slice x32, local copies, waits for them, and re-layouts, on_device(): partial_value = lax.map(one_source, (piece, sources))  18.6 us
    add x1, other arithmetic, channelize(): filtered + pfb_taps[tap_index] * frames[..., tap_index:tap_index + frames...  8.62 us
  transfers between devices with their start and end apart: 2, of which 2 were waited for; matrix products, arithmetic and copies ran while one was open for 2% of the time, Pallas kernels for 0%

commit v1 on v0

v1 whole, which is shorter than its diff:
```python
import functools
import math

import jax
import jax.numpy as jnp
import numpy as np
from jax import lax
from jax.experimental import pallas as pl
from jax.experimental.pallas import tpu as pltpu
from jax.sharding import PartitionSpec as P

FINE = 256
COARSE = 4
TAPS = 16
SHIFTS = 16
NBOX = 8
MAXW = 32
TOUT = 768
FRAMES = TOUT + SHIFTS - 1
ROWS = 784
PIECE = 256
PIECES = TOUT // PIECE
CUTS = ((0, 272), (272, 256), (528, 256))
BLOCK = 112
MESH = pl.DeviceIdType.MESH
BF16 = jnp.bfloat16
F32 = jnp.float32


def dft_tables():
    position = np.arange(FINE)
    angles = (position[:, None] * position[None, :] % FINE) * (2.0 * math.pi / FINE)
    cosine = np.cos(angles) / math.sqrt(FINE)
    sine = np.sin(angles) / math.sqrt(FINE)
    table = np.concatenate(
        [np.concatenate([cosine, -sine], 1), np.concatenate([sine, cosine], 1)], 0
    ).astype(np.float32)
    high = table.astype(BF16)
    low = (table - high.astype(np.float32)).astype(BF16)
    return np.stack([high, low])


def channelize(volt_ref, taps_ref, table, frames, powers, own):
    frames[:, ROWS - 8 :, :] = jnp.zeros((2, frames.shape[1] - ROWS + 8, FINE), F32)
    for part in range(2):
        frames[part, 0 : volt_ref.shape[1], :] = volt_ref[part].astype(F32)
    taps = taps_ref[...]

    def step(index, total):
        start = pl.multiple_of(index * BLOCK, 16)
        halves = []
        for part in range(2):
            window = frames[part, pl.ds(start, BLOCK + TAPS), :]
            value = taps[0:1] * window[0:BLOCK]
            for tap in range(1, TAPS):
                value = value + taps[tap : tap + 1] * window[tap : tap + BLOCK]
            halves.append(value)
        stacked = jnp.concatenate(halves, axis=1)
        high = stacked.astype(BF16)
        low = (stacked - high.astype(F32)).astype(BF16)
        spectra = (
            jnp.dot(high, table[0], preferred_element_type=F32)
            + jnp.dot(low, table[0], preferred_element_type=F32)
            + jnp.dot(high, table[1], preferred_element_type=F32)
        )
        power = spectra[:, :FINE] ** 2 + spectra[:, FINE:] ** 2
        frame = start + lax.broadcasted_iota(jnp.int32, (BLOCK, FINE), 0)
        power = jnp.where(frame < FRAMES, power, 0.0)
        powers[pl.ds(start, BLOCK), :] = power
        return total + jnp.sum(power, axis=0, keepdims=True)

    total = lax.fori_loop(0, ROWS // BLOCK, step, jnp.zeros((1, FINE), F32))
    mean = total * (1.0 / FRAMES)

    @pl.loop(0, ROWS // BLOCK)
    def _(index):
        rows = pl.ds(pl.multiple_of(index * BLOCK, 16), BLOCK)
        own[0, rows, :] = (powers[rows, :] - mean).astype(BF16)


def search_kernel(
    beams,
    volt_ref,
    taps_ref,
    table_hbm,
    delays_hbm,
    assign_ref,
    out_ref,
    table,
    delays,
    frames,
    powers,
    slabs,
    onehot,
    shifted,
    total,
    outbox,
    load_sem,
    ring_send,
    ring_recv,
    block_send,
    block_recv,
    local_sem,
):
    me = lax.axis_index("beam")
    sub = lax.axis_index("sub")
    subs = COARSE
    left, right = lax.rem(sub + subs - 1, subs), lax.rem(sub + 1, subs)

    barrier = pltpu.get_barrier_semaphore()
    for side in (left, right):
        pl.semaphore_signal(barrier, inc=1, device_id={"sub": side}, device_id_type=MESH)

    @pl.loop(1, beams)
    def _(offset):
        peer = lax.rem(me + offset, beams)
        pl.semaphore_signal(barrier, inc=1, device_id={"beam": peer}, device_id_type=MESH)

    table_copy = pltpu.make_async_copy(table_hbm, table, load_sem.at[0])
    table_copy.start()
    delays_copy = pltpu.make_async_copy(
        delays_hbm.at[:, pl.ds(pl.multiple_of(sub * 16, 16), 16), :], delays, load_sem.at[1]
    )
    delays_copy.start()
    table_copy.wait()
    channelize(volt_ref, taps_ref, table, frames, powers, slabs)
    pl.semaphore_wait(barrier, 2 + beams - 1)

    def ring(source, target, first, count, side, which):
        return pltpu.make_async_remote_copy(
            src_ref=slabs.at[source, pl.ds(first, count)],
            dst_ref=slabs.at[target, pl.ds(first, count)],
            send_sem=ring_send.at[which],
            recv_sem=ring_recv.at[which],
            device_id={"sub": side},
            device_id_type=MESH,
        )

    near, far = [], []
    for piece, (first, count) in enumerate(CUTS):
        near.append(
            (
                ring(0, 1, first, count, right, 4 * piece),
                ring(0, 2, first, count, left, 4 * piece + 1),
            )
        )
        half = 128
        far.append(
            (
                ring(1, 3, first, half, right, 4 * piece + 2),
                ring(2, 3, first + half, count - half, left, 4 * piece + 3),
            )
        )

    def pass_on(piece):
        for arrived, onward in zip(near[piece], far[piece]):
            arrived.wait_recv()
            onward.start()

    for copy in near[0] + near[1]:
        copy.start()

    delays_copy.wait()

    @pl.loop(0, beams)
    def _(owner):
        rows = pl.ds(pl.multiple_of(owner * 16, 16), 16)
        for slot, hop in enumerate((0, subs - 1, 1, 2)):
            coarse = lax.rem(sub + hop, subs)
            lanes = pl.ds(pl.multiple_of(coarse * FINE, FINE), FINE)
            lookup = delays[assign_ref[me, owner], :, lanes].astype(F32).astype(BF16)
            for shift in range(SHIFTS):
                onehot[slot, rows, shift * FINE : (shift + 1) * FINE] = jnp.where(
                    lookup == BF16(shift), BF16(1), BF16(0)
                )

    def shift_rows(slot, piece):
        @pl.loop(0, PIECE // 32)
        def _(index):
            start = pl.multiple_of(index * 32, 32)
            window = slabs[slot, pl.ds(piece * PIECE + start, 48), :]
            for shift in range(SHIFTS):
                shifted[pl.ds(start, 32), shift * FINE : (shift + 1) * FINE] = window[
                    shift : shift + 32
                ]

    def add_slot(slot, piece, rows):
        product = lax.dot_general(
            onehot[slot, rows, :],
            shifted[...],
            (((1,), (1,)), ((), ())),
            preferred_element_type=F32,
        )
        if slot == 0:
            total[piece, rows, :] = product
        else:
            total[piece, rows, :] += product

    every = pl.ds(0, beams * 16)
    half_span = beams // 2
    scale = 1.0 / math.sqrt(COARSE * FINE)

    def block_copy(piece, owner):
        return pltpu.make_async_remote_copy(
            src_ref=outbox.at[piece, owner],
            dst_ref=out_ref.at[piece, me],
            send_sem=block_send.at[piece],
            recv_sem=block_recv.at[piece],
            device_id={"beam": owner},
            device_id_type=MESH,
        )

    def deliver(piece, part):
        rows = pl.ds(part * half_span * 16, half_span * 16)
        series = (total[piece, rows, :] * scale).astype(BF16)
        outbox[piece, pl.ds(part * half_span, half_span)] = series.reshape(
            half_span, 16, PIECE
        )

        @pl.loop(0, half_span)
        def _(offset):
            owner = part * half_span + lax.rem(me + offset, half_span)

            @pl.when(owner != me)
            def _():
                block_copy(piece, owner).start()

            @pl.when(owner == me)
            def _():
                pltpu.make_async_copy(
                    outbox.at[piece, me], out_ref.at[piece, me], local_sem.at[piece]
                ).start()

    for piece in range(PIECES):
        if piece == 1:
            pass_on(0)
            for copy in near[2]:
                copy.start()
        shift_rows(0, piece)
        add_slot(0, piece, every)
    pass_on(1)

    for piece in range(PIECES):
        for slot in (1, 2, 3):
            if piece == 0 and slot == 3:
                pass_on(2)
            if slot == 3:
                for copy in far[piece]:
                    copy.wait_recv()
            shift_rows(slot, piece)
            if slot < 3:
                add_slot(slot, piece, every)
            else:
                for part in range(2):
                    add_slot(slot, piece, pl.ds(part * half_span * 16, half_span * 16))
                    deliver(piece, part)

    for piece in range(PIECES):
        pltpu.make_async_copy(
            outbox.at[piece, me], out_ref.at[piece, me], local_sem.at[piece]
        ).wait()
        others = pltpu.make_async_remote_copy(
            src_ref=outbox.at[piece, pl.ds(0, beams - 1)],
            dst_ref=out_ref.at[piece, pl.ds(0, beams - 1)],
            send_sem=block_send.at[piece],
            recv_sem=block_recv.at[piece],
            device_id={"beam": me},
            device_id_type=MESH,
        )
        others.wait_recv()
        others.wait_send()
    for piece in range(PIECES):
        for copy in near[piece] + far[piece]:
            copy.wait_send()


def boxcar_kernel(widths_ref, blocks_ref, triangle_ref, series_ref, snr_ref, prefix):
    beams = blocks_ref.shape[1]
    rows = beams * 16
    for piece in range(PIECES):
        series_ref[0, :, :, piece * PIECE : (piece + 1) * PIECE] = blocks_ref[piece]
    series = series_ref[0].reshape(rows, TOUT)
    sums = lax.dot_general(
        triangle_ref[...], series, (((1,), (1,)), ((), ())), preferred_element_type=F32
    )
    lane_tiles = rows // 128
    for tile in range(lane_tiles):
        prefix[tile] = sums[:, tile * 128 : (tile + 1) * 128]
    for tile in range(lane_tiles):
        best = []
        for box in range(NBOX):
            width = widths_ref[box]

            def step(index, best_so_far):
                start = pl.multiple_of(index * 64, 64)
                window = prefix[tile, pl.ds(start + width, 64), :] - prefix[
                    tile, pl.ds(start, 64), :
                ]
                return jnp.maximum(best_so_far, jnp.max(window.reshape(8, 8, 128), axis=0))

            top = lax.fori_loop(0, TOUT // 64, step, jnp.full((8, 128), -jnp.inf, F32))
            top = jnp.max(top, axis=0, keepdims=True)
            best.append(top / jnp.sqrt(jnp.full((1, 128), width, jnp.int32).astype(F32)))
        best = jnp.concatenate(best, axis=0)
        snr_ref[0, pl.ds(tile * 8, 8), :, :] = best.T.reshape(8, 16, NBOX)


def on_device(beams, voltages, pfb_taps, delays, assignment, widths):
    span = delays.shape[0] // beams
    own_span = span // COARSE
    assert own_span == 16
    vmem = pl.BlockSpec(memory_space=pltpu.VMEM)
    smem = pl.BlockSpec(memory_space=pltpu.SMEM)
    anywhere = pl.BlockSpec(memory_space=pl.ANY)
    chans = COARSE * FINE
    rows = beams * own_span
    blocks = pl.pallas_call(
        functools.partial(search_kernel, beams),
        out_shape=jax.ShapeDtypeStruct((PIECES, beams, own_span, PIECE), BF16),
        in_specs=[vmem, vmem, anywhere, anywhere, smem],
        out_specs=anywhere,
        scratch_shapes=[
            pltpu.VMEM((2, 2 * FINE, 2 * FINE), BF16),
            pltpu.VMEM((beams, own_span, chans), jnp.int32),
            pltpu.VMEM((2, ROWS + 32, FINE), F32),
            pltpu.VMEM((ROWS, FINE), F32),
            pltpu.VMEM((COARSE, ROWS, FINE), BF16),
            pltpu.VMEM((COARSE, rows, SHIFTS * FINE), BF16),
            pltpu.VMEM((PIECE, SHIFTS * FINE), BF16),
            pltpu.VMEM((PIECES, rows, PIECE), F32),
            pltpu.VMEM((PIECES, beams, own_span, PIECE), BF16),
            pltpu.SemaphoreType.DMA((2,)),
            pltpu.SemaphoreType.DMA((4 * PIECES,)),
            pltpu.SemaphoreType.DMA((4 * PIECES,)),
            pltpu.SemaphoreType.DMA((PIECES,)),
            pltpu.SemaphoreType.DMA((PIECES,)),
            pltpu.SemaphoreType.DMA((PIECES,)),
        ],
        compiler_params=pltpu.CompilerParams(
            collective_id=0, has_side_effects=True, vmem_limit_bytes=56 << 20
        ),
    )(
        voltages.reshape(2, voltages.shape[-2], FINE),
        pfb_taps,
        jnp.asarray(dft_tables()),
        delays.reshape(beams, span, chans),
        assignment,
    )
    edge = np.arange(TOUT + MAXW)
    triangle = jnp.asarray((np.arange(TOUT)[None, :] < edge[:, None]).astype(BF16))
    return pl.pallas_call(
        boxcar_kernel,
        out_shape=(
            jax.ShapeDtypeStruct((1, beams, own_span, TOUT), BF16),
            jax.ShapeDtypeStruct((1, beams, own_span, NBOX), F32),
        ),
        in_specs=[smem, vmem, vmem],
        out_specs=(vmem, vmem),
        scratch_shapes=[pltpu.VMEM((rows // 128, TOUT + MAXW, 128), F32)],
        compiler_params=pltpu.CompilerParams(vmem_limit_bytes=32 << 20),
    )(widths, blocks, triangle)


def solution(mesh):
    in_specs = (P(None, "beam", "sub", None, None), P(), P(), P(), P())
    out_specs = (P("beam", None, "sub", None), P("beam", None, "sub", None))
    return jax.shard_map(
        functools.partial(on_device, mesh.shape["beam"]),
        mesh=mesh,
        in_specs=in_specs,
        out_specs=out_specs,
        check_vma=False,
    )
```

time: 427 us -> 66.4 us (0.16)
  waiting for transfers between devices: 120 us -> 0 us
  loops' own time: 83.7 us -> 0 us
  other arithmetic: 73.4 us -> 0 us
  matrix products: 66.6 us -> 0 us
  Pallas kernels: 0 us -> 61.4 us
  local copies, waits for them, and re-layouts: 65.4 us -> 4.18 us
  between operations: 14.2 us -> 0.68 us
    another operation x1 -> x0, loops' own time: 83.7 us -> none  [on_device(): partial_value = lax.map(one_source, (piece, sources))]
    dot_general x34 -> x0, matrix products: 66.6 us -> none  [the longest x32 55.9 us: delay_sum(): jnp.einsum('src,tc->srt', table, power_rows, preferred_element_type=jnp.f...]
    all_gather x1 -> x0, waiting for transfers between devices: 65.4 us -> none  [on_device(): piece = lax.all_gather(fine_power[None], 'beam', axis=0, tiled=True)]
    dynamic_slice x97 -> x0, local copies, waits for them, and re-layouts: 61.6 us -> none  [the longest x32 40.8 us: one_source(): offset = assignment[anchor, my_beam] * dm_span]
    pallas_call x0 -> x2, Pallas kernels: none -> 61.4 us  [the longest x1 54.6 us: on_device(): pl.pallas_call(functools.partial(search_kernel, beams), out_shape=jax.Sha...]
    reduce_scatter x1 -> x0, waiting for transfers between devices: 54.8 us -> none  [on_device(): lax.psum_scatter(partial_value, 'sub', scatter_dimension=1, tiled=True)]
    dynamic_update_slice x32 -> x0, other arithmetic: 48.4 us -> none  [on_device(): partial_value = lax.map(one_source, (piece, sources))]
    add x2 -> x0, other arithmetic: 8.62 us -> none  [the longest x1 8.62 us: channelize(): filtered + pfb_taps[tap_index] * frames[..., tap_index:tap_index + frames...]
  transfers between devices with their start and end apart: 2 -> 0, of which waited for: 2 -> 0; matrix products, arithmetic and copies ran while one was open for 2% -> 0% of each run, Pallas kernels for 0% -> 0%
where the time goes in v1:
time: 66.4 us; the launch traced here: 66.2 us
  Pallas kernels  61.4 us (92%)
  local copies, waits for them, and re-layouts  4.18 us (6%)
  between operations  0.68 us (1%)
    pallas_call x1, Pallas kernels, on_device(): pl.pallas_call(functools.partial(search_kernel, beams), out_shape=jax.Sha...  54.6 us
    pallas_call x1, Pallas kernels, on_device(): pl.pallas_call(boxcar_kernel, out_shape=(jax.ShapeDtypeStruct((1, beams,...  6.72 us
    unnamed x7, local copies, waits for them, and re-layouts  3.39 us

profile of v1, /device:TPU:1, one launch (start us, length us, event | category | flops | bytes accessed | tf_op | source)
XLA Modules:
  0.0 66.2 jit_solution(16671395859669237250)
XLA Ops:
  0.6 0.0 copy-start.1
  0.6 0.0 copy-start.2
  0.7 2.3 %copy.12 = bf16[2,1,1,798,256]{4,3,0,2,1:T(8,128)(2,1)} copy(bf16[2,1,1,798,256]{4,0,3,2,1:T(2,128)(2,1)} %param.7) | data formatting | bytes 1634304 | tf_op args[0]
  2.9 54.6 %shard_map.86.blocks_ref = bf16[3,32,16,256]{3,2,1,0:T(8,128)(2,1)} custom-call(bf16[2,798,256]{2,1,0:T(8,128)(2,1)} %bitcast.5, f32[16,256]{1,0:T(8,128)} %taps_ref.1, bf16[2,512,512]{2,1,0:T(8,128)(2,1)} %constant.4.clone.table_hbm, s32[32,64,1024]{2,1,0:T(8,128)} %bitcast.4, s32[32,32]{1,0:T(8,128)} %assign_ref.1), custom_call_target="tpu_custom_call" | custom-call | tf_op jit(solution)/shard_map/pallas_call | solution.py:317
  57.6 0.0 copy-done.1
  57.6 0.0 copy-done.2
  57.6 0.0 copy-start
  57.6 1.1 %copy-done = bf16[3,32,16,256]{3,2,1,0:T(8,128)(2,1)S(1)} copy-done((bf16[3,32,16,256]{3,2,1,0:T(8,128)(2,1)S(1)}, bf16[3,32,16,256]{3,2,1,0:T(8,128)(2,1)}, u32[]{:S(2)}) %copy-start) | copy-done | bytes 786456
  58.7 6.7 %shard_map.87 = (bf16[1,32,16,768]{3,2,1,0:T(8,128)(2,1)}, f32[1,32,16,8]{3,2,1,0:T(8,128)S(1)}) custom-call(s32[8]{0:T(128)S(1)} %copy-done.2, bf16[3,32,16,256]{3,2,1,0:T(8,128)(2,1)S(1)} %copy-done, bf16[800,768]{1,0:T(8,128)(2,1)S(1)} %copy-done.1), custom_call_target="tpu_custom_call" | custom-call | tf_op jit(solution)/shard_map/pallas_call | solution.py:351
  65.4 0.8 %copy.10 = f32[1,32,16,8]{1,3,2,0:T(8,128)} copy(f32[1,32,16,8]{3,2,1,0:T(8,128)S(1)} %get-tuple-element.3) | data formatting | bytes 32768 | tf_op jit(solution)/shard_map/pallas_call | solution.py:351
Async XLA Ops:
  0.6 56.9 %copy-start.1 = (bf16[800,768]{1,0:T(8,128)(2,1)S(1)}, bf16[800,768]{1,0:T(8,128)(2,1)}, u32[]{:S(2)}) copy-start(bf16[800,768]{1,0:T(8,128)(2,1)} %constant.5.clone.triangle_ref) | copy-start | bytes 3686404
  0.6 56.9 %copy-start.2 = (s32[8]{0:T(128)S(1)}, s32[8]{0:T(128)}, u32[]{:S(2)}) copy-start(s32[8]{0:T(128)} %widths_ref.1) | copy-start | bytes 100
  57.6 1.1 %copy-start = (bf16[3,32,16,256]{3,2,1,0:T(8,128)(2,1)S(1)}, bf16[3,32,16,256]{3,2,1,0:T(8,128)(2,1)}, u32[]{:S(2)}) copy-start(bf16[3,32,16,256]{3,2,1,0:T(8,128)(2,1)} %shard_map.86.blocks_ref) | copy-start | bytes 2359300

commit v2 on v1

v2 whole, which is shorter than its diff:
```python
import functools
import math

import jax
import jax.numpy as jnp
import numpy as np
from jax import lax
from jax.experimental import pallas as pl
from jax.experimental.pallas import tpu as pltpu
from jax.sharding import PartitionSpec as P

FINE = 256
COARSE = 4
TAPS = 16
SHIFTS = 16
NBOX = 8
MAXW = 32
TOUT = 768
FRAMES = TOUT + SHIFTS - 1
ROWS = 784
PIECE = 256
PIECES = TOUT // PIECE
CUTS = ((0, 272), (272, 256), (528, 256))
BLOCK = 392
MESH = pl.DeviceIdType.MESH
BF16 = jnp.bfloat16
F32 = jnp.float32


def dft_table():
    position = np.arange(FINE)
    angles = (position[:, None] * position[None, :] % FINE) * (2.0 * math.pi / FINE)
    cosine = np.cos(angles) / math.sqrt(FINE)
    sine = np.sin(angles) / math.sqrt(FINE)
    table = np.concatenate(
        [np.concatenate([cosine, -sine], 1), np.concatenate([sine, cosine], 1)], 0
    ).astype(np.float32)
    return table


def channelize(volt_ref, taps_ref, table, split, table_copy, frames, powers, own):
    count = volt_ref.shape[0]
    frames[count:, :] = jnp.zeros((frames.shape[0] - count, 128), F32)
    chunk = count // 7

    @pl.loop(0, 7)
    def _(index):
        rows = pl.ds(pl.multiple_of(index * chunk, 8), chunk)
        frames[rows, :] = volt_ref[rows, :].astype(F32)

    taps = taps_ref[...]
    table_copy.wait()
    table_high = table[...].astype(BF16)
    table_low = (table[...] - table_high.astype(F32)).astype(BF16)
    split[0] = table_high
    split[1] = table_low

    def step(index, total):
        start = pl.multiple_of(index * BLOCK, 8)
        halves = []
        for part in range(2):
            for side in range(2):
                weights = taps[:, side * 128 : (side + 1) * 128]
                value = 0.0
                for tap in range(TAPS):
                    first = 4 * (start + tap) + 2 * side + part
                    value = value + weights[tap : tap + 1] * frames[
                        pl.ds(first, BLOCK, stride=4), :
                    ]
                halves.append(value)
        stacked = jnp.concatenate(halves, axis=1)
        high = stacked.astype(BF16)
        low = (stacked - high.astype(F32)).astype(BF16)
        spectra = (
            jnp.dot(high, split[0], preferred_element_type=F32)
            + jnp.dot(low, split[0], preferred_element_type=F32)
            + jnp.dot(high, split[1], preferred_element_type=F32)
        )
        power = spectra[:, :FINE] ** 2 + spectra[:, FINE:] ** 2
        frame = start + lax.broadcasted_iota(jnp.int32, (BLOCK, FINE), 0)
        power = jnp.where(frame < FRAMES, power, 0.0)
        powers[pl.ds(start, BLOCK), :] = power
        return total + jnp.sum(power, axis=0, keepdims=True)

    total = lax.fori_loop(0, ROWS // BLOCK, step, jnp.zeros((1, FINE), F32))
    mean = total * (1.0 / FRAMES)

    @pl.loop(0, 7)
    def _(index):
        rows = pl.ds(pl.multiple_of(index * (ROWS // 7), 16), ROWS // 7)
        own[0, rows, :] = (powers[rows, :] - mean).astype(BF16)


def search_kernel(
    beams,
    volt_ref,
    taps_ref,
    table_hbm,
    delays_hbm,
    assign_ref,
    widths_ref,
    series_ref,
    snr_ref,
    table,
    split,
    delays,
    lookups,
    frames,
    powers,
    slabs,
    total,
    outbox,
    prefix,
    snr_out,
    snr_in,
    plane_sem,
    load_sem,
    ring_send,
    ring_recv,
    block_send,
    block_recv,
    local_sem,
    snr_send,
    snr_recv,
):
    me = lax.axis_index("beam")
    sub = lax.axis_index("sub")
    subs = COARSE
    left, right = lax.rem(sub + subs - 1, subs), lax.rem(sub + 1, subs)

    barrier = pltpu.get_barrier_semaphore()
    for side in (left, right):
        pl.semaphore_signal(barrier, inc=1, device_id={"sub": side}, device_id_type=MESH)

    line = 8
    planes = beams // line
    plane, place = lax.div(me, line), lax.rem(me, line)
    others_of_place = [
        lax.rem(plane + hop, planes) * line + place for hop in range(1, planes)
    ]
    others_of_plane = [
        plane * line + lax.rem(place + hop, line) for hop in range(1, line)
    ]
    hops = [(0, 0), (0, 1), (0, 3), (1, 0), (3, 0), (0, 2), (2, 0), (1, 1)]
    hops += [(3, 3), (1, 3), (3, 1), (1, 2), (2, 1), (3, 2), (2, 3), (2, 2)]
    hops = [hop for hop in reversed(hops) if hop[0] < planes]
    others = [
        lax.rem(plane + far, planes) * line
        + lax.rem(place + 2 * near, line)
        + (core if core == 0 else 1 - 2 * lax.rem(place, 2))
        for far, near in hops
        for core in range(2)
        if (far, near, core) != (0, 0, 0)
    ]
    for peer in others_of_place + others_of_plane:
        pl.semaphore_signal(barrier, inc=1, device_id={"beam": peer}, device_id_type=MESH)

    table_copy = pltpu.make_async_copy(table_hbm, table, load_sem.at[0])
    table_copy.start()
    delays_copy = pltpu.make_async_copy(
        delays_hbm.at[:, pl.ds(pl.multiple_of(sub * 16, 16), 16), :], delays, load_sem.at[1]
    )
    delays_copy.start()
    channelize(volt_ref, taps_ref, table, split, table_copy, frames, powers, slabs)
    pl.semaphore_wait(barrier, 2 + planes - 1 + line - 1)
    for peer in others_of_place:
        pl.semaphore_signal(plane_sem, inc=1, device_id={"beam": peer}, device_id_type=MESH)

    def ring(source, target, first, count, side, which):
        return pltpu.make_async_remote_copy(
            src_ref=slabs.at[source, pl.ds(first, count)],
            dst_ref=slabs.at[target, pl.ds(first, count)],
            send_sem=ring_send.at[which],
            recv_sem=ring_recv.at[which],
            device_id={"sub": side},
            device_id_type=MESH,
        )

    near, far = [], []
    for piece, (first, count) in enumerate(CUTS):
        near.append(
            (
                ring(0, 1, first, count, right, 4 * piece),
                ring(0, 2, first, count, left, 4 * piece + 1),
            )
        )
        half = 128
        far.append(
            (
                ring(1, 3, first, half, right, 4 * piece + 2),
                ring(2, 3, first + half, count - half, left, 4 * piece + 3),
            )
        )

    def pass_on(piece):
        for arrived, onward in zip(near[piece], far[piece]):
            arrived.wait_recv()
            onward.start()

    for copy in near[0]:
        copy.start()
    delays_copy.wait()

    @pl.loop(0, beams)
    def _(owner):
        rows = pl.ds(pl.multiple_of(owner * 16, 16), 16)
        for slot, hop in enumerate((0, subs - 1, 1, 2)):
            coarse = lax.rem(sub + hop, subs)
            lanes = pl.ds(pl.multiple_of(coarse * FINE, FINE), FINE)
            lookup = delays[assign_ref[me, owner], :, lanes]
            lookups[slot, rows, :] = lookup.astype(F32).astype(BF16)

    def product(slot, piece):
        start = pl.multiple_of(piece * PIECE, PIECE)
        window = slabs[slot, pl.ds(start, PIECE + SHIFTS), :]
        shifted = jnp.concatenate(
            [window[shift : shift + PIECE] for shift in range(SHIFTS)], axis=1
        )
        lookup = lookups[slot]
        onehot = jnp.concatenate(
            [jnp.where(lookup == BF16(shift), BF16(1), BF16(0)) for shift in range(SHIFTS)],
            axis=1,
        )
        return lax.dot_general(
            onehot, shifted, (((1,), (1,)), ((), ())), preferred_element_type=F32
        )

    scale = 1.0 / math.sqrt(COARSE * FINE)

    def columns(piece):
        return pl.ds(pl.multiple_of(piece * PIECE, PIECE), PIECE)

    def block_copy(piece, owner):
        return pltpu.make_async_remote_copy(
            src_ref=outbox.at[piece, owner],
            dst_ref=series_ref.at[0, me, :, columns(piece)],
            send_sem=block_send.at[piece],
            recv_sem=block_recv.at[piece],
            device_id={"beam": owner},
            device_id_type=MESH,
        )

    def own_copy(piece):
        return pltpu.make_async_copy(
            outbox.at[piece, me], series_ref.at[0, me, :, columns(piece)], local_sem.at[piece]
        )

    def deliver(piece):
        series = (total[piece] * scale).astype(BF16)
        outbox[piece] = series.reshape(beams, 16, PIECE)
        own_copy(piece).start()

        for owner in others:
            block_copy(piece, owner).start()

        count = PIECE + 16
        triangle = jnp.where(
            lax.broadcasted_iota(jnp.int32, (count, PIECE), 1)
            < lax.broadcasted_iota(jnp.int32, (count, PIECE), 0),
            1.0,
            0.0,
        ).astype(BF16)
        sums = lax.dot_general(
            triangle, series, (((1,), (1,)), ((), ())), preferred_element_type=F32
        )
        start = pl.multiple_of(piece * PIECE, PIECE)
        for tile in range(lane_tiles):
            carry = prefix[tile, pl.ds(start, 8), :][0:1]
            prefix[tile, pl.ds(start, count), :] = (
                sums[:, tile * 128 : (tile + 1) * 128] + carry
            )

    lane_tiles = beams * 16 // 128
    prefix[:, 0:8, :] = jnp.zeros((lane_tiles, 8, 128), F32)
    @pl.loop(0, PIECES)
    def _(piece):
        @pl.when(piece == 2)
        def _():
            for copy in near[1]:
                copy.start()

        total[piece] = product(0, piece)

    pass_on(0)

    @pl.loop(0, 3 * PIECES)
    def _(step):
        piece = lax.div(step, 3)
        slot = 1 + lax.rem(step, 3)

        @pl.when(step == 2)
        def _():
            for copy in near[2]:
                copy.start()
            pl.semaphore_wait(plane_sem, planes - 1)

        for later in range(1, PIECES):

            @pl.when(step == 3 * later)
            def _():
                pass_on(later)

        for now in range(PIECES):

            @pl.when(step == 3 * now + 2)
            def _():
                for copy in far[now]:
                    copy.wait_recv()

        total[piece] += product(slot, piece)

        @pl.when(slot == 3)
        def _():
            deliver(piece)

    boxcars(widths_ref, prefix, snr_out)
    snr_in[pl.ds(me, 1)] = snr_out[pl.ds(me, 1)]

    for owner in others:
        pltpu.make_async_remote_copy(
            src_ref=snr_out.at[owner],
            dst_ref=snr_in.at[me],
            send_sem=snr_send,
            recv_sem=snr_recv,
            device_id={"beam": owner},
            device_id_type=MESH,
        ).start()

    for piece in range(PIECES):
        own_copy(piece).wait()
        all_blocks = pltpu.make_async_remote_copy(
            src_ref=outbox.at[piece, pl.ds(0, beams - 1)],
            dst_ref=series_ref.at[0, pl.ds(0, beams - 1), :, columns(piece)],
            send_sem=block_send.at[piece],
            recv_sem=block_recv.at[piece],
            device_id={"beam": me},
            device_id_type=MESH,
        )
        all_blocks.wait_recv()
        all_blocks.wait_send()
    all_snr = pltpu.make_async_remote_copy(
        src_ref=snr_out.at[pl.ds(0, beams - 1)],
        dst_ref=snr_in.at[pl.ds(0, beams - 1)],
        send_sem=snr_send,
        recv_sem=snr_recv,
        device_id={"beam": me},
        device_id_type=MESH,
    )
    all_snr.wait_recv()
    all_snr.wait_send()
    for piece in range(PIECES):
        for copy in near[piece] + far[piece]:
            copy.wait_send()
    snr_ref[...] = jnp.transpose(snr_in[:, :, 0:16], (2, 1, 0))


def boxcars(widths_ref, prefix, snr_out):
    lane_tiles = prefix.shape[0]
    block = 64
    widths = [widths_ref[box] for box in range(NBOX)]
    root = [
        1.0 / jnp.sqrt(jnp.full((1, 128), width, jnp.int32).astype(F32)) for width in widths
    ]
    tail = prefix.shape[1] - TOUT
    for tile in range(lane_tiles):
        prefix[tile, TOUT:, :] = jnp.broadcast_to(
            prefix[tile, TOUT : TOUT + 8, :][0:1], (tail, 128)
        )

    @pl.loop(0, lane_tiles)
    def _(tile):
        def step(index, best):
            start = pl.multiple_of(index * block, block)
            base = prefix[tile, pl.ds(start, block), :]
            out = []
            for box in range(NBOX):
                gain = prefix[tile, pl.ds(start + widths[box], block), :] - base
                top = jnp.max(gain.reshape(block // 8, 8, 128), axis=0)
                out.append(jnp.maximum(best[box], top))
            return tuple(out)

        best = lax.fori_loop(
            0, TOUT // block, step, tuple(jnp.full((8, 128), -jnp.inf, F32) for _ in range(NBOX))
        )
        best = jnp.concatenate(
            [jnp.max(top, axis=0, keepdims=True) * root[box] for box, top in enumerate(best)],
            axis=0,
        )
        for owner in range(8):
            snr_out[tile * 8 + owner] = pltpu.roll(best, (128 - 16 * owner) % 128, 1)


def on_device(beams, voltages, pfb_taps, delays, assignment, widths):
    span = delays.shape[0] // beams
    own_span = span // COARSE
    assert own_span == 16
    vmem = pl.BlockSpec(memory_space=pltpu.VMEM)
    smem = pl.BlockSpec(memory_space=pltpu.SMEM)
    anywhere = pl.BlockSpec(memory_space=pl.ANY)
    chans = COARSE * FINE
    rows = beams * own_span
    series, snr = pl.pallas_call(
        functools.partial(search_kernel, beams),
        out_shape=(
            jax.ShapeDtypeStruct((1, beams, own_span, TOUT), BF16),
            jax.ShapeDtypeStruct((own_span, NBOX, beams), F32),
        ),
        in_specs=[vmem, vmem, anywhere, anywhere, smem, smem],
        out_specs=(anywhere, vmem),
        scratch_shapes=[
            pltpu.VMEM((2 * FINE, 2 * FINE), F32),
            pltpu.VMEM((2, 2 * FINE, 2 * FINE), BF16),
            pltpu.VMEM((beams, own_span, chans), jnp.int32),
            pltpu.VMEM((COARSE, rows, FINE), BF16),
            pltpu.VMEM((4 * (ROWS + 16), 128), F32),
            pltpu.VMEM((ROWS, FINE), F32),
            pltpu.VMEM((COARSE, ROWS, FINE), BF16),
            pltpu.VMEM((PIECES, rows, PIECE), F32),
            pltpu.VMEM((PIECES, beams, own_span, PIECE), BF16),
            pltpu.VMEM((rows // 128, TOUT + MAXW + 8, 128), F32),
            pltpu.VMEM((beams, NBOX, 128), F32),
            pltpu.VMEM((beams, NBOX, 128), F32),
            pltpu.SemaphoreType.REGULAR,
            pltpu.SemaphoreType.DMA((2,)),
            pltpu.SemaphoreType.DMA((4 * PIECES,)),
            pltpu.SemaphoreType.DMA((4 * PIECES,)),
            pltpu.SemaphoreType.DMA((PIECES,)),
            pltpu.SemaphoreType.DMA((PIECES,)),
            pltpu.SemaphoreType.DMA((PIECES,)),
            pltpu.SemaphoreType.DMA,
            pltpu.SemaphoreType.DMA,
        ],
        compiler_params=pltpu.CompilerParams(
            collective_id=0, has_side_effects=True, vmem_limit_bytes=60 << 20
        ),
    )(
        voltages.reshape(2, -1, 2, 128).transpose(1, 2, 0, 3).reshape(-1, 128),
        pfb_taps,
        jnp.asarray(dft_table()),
        delays.reshape(beams, span, chans),
        assignment,
        widths,
    )
    return series, snr.transpose(2, 0, 1)[None]


def solution(mesh):
    in_specs = (P(None, "beam", "sub", None, None), P(), P(), P(), P())
    out_specs = (P("beam", None, "sub", None), P("beam", None, "sub", None))
    return jax.shard_map(
        functools.partial(on_device, mesh.shape["beam"]),
        mesh=mesh,
        in_specs=in_specs,
        out_specs=out_specs,
        check_vma=False,
    )
```

time: 66.4 us -> 46.9 us (0.71)
  Pallas kernels: 61.4 us -> 42.5 us
    pallas_call x2 -> x1, Pallas kernels: 61.4 us -> 42.5 us  [on_device(): pl.pallas_call(functools.partial(search_kernel, beams), out_shape=(jax.Sh...]
    pallas_call x1 -> x0, local copies, waits for them, and re-layouts: 0.78 us -> none  [on_device(): pl.pallas_call(boxcar_kernel, out_shape=(jax.ShapeDtypeStruct((1, beams,...]
    unnamed x7 -> x2, local copies, waits for them, and re-layouts: 3.39 us -> 3.54 us
where the time goes in v2:
time: 46.9 us; the launch traced here: 46.7 us
  Pallas kernels  42.5 us (91%)
  local copies, waits for them, and re-layouts  3.54 us (8%)
  between operations  0.64 us (1%)
    pallas_call x1, Pallas kernels, on_device(): pl.pallas_call(functools.partial(search_kernel, beams), out_shape=(jax.Sh...  42.5 us
    unnamed x2, local copies, waits for them, and re-layouts  3.54 us

profile of v2, /device:TPU:1, one launch (start us, length us, event | category | flops | bytes accessed | tf_op | source)
XLA Modules:
  0.0 46.7 jit_solution(9159750598712233702)
XLA Ops:
  0.6 42.5 %shard_map.77 = (bf16[1,32,16,768]{3,2,1,0:T(8,128)(2,1)}, f32[16,8,32]{2,1,0:T(8,128)}) custom-call(bf16[3192,128]{1,0:T(8,128)(2,1)} %bitcast.10, f32[16,256]{1,0:T(8,128)} %taps_ref.1, f32[512,512]{1,0:T(8,128)} %constant.2.clone.table_hbm, s32[32,64,1024]{2,1,0:T(8,128)} %bitcast.9, s32[32,32]{1,0:T(8,128)} %assign_ref.1, s32[8]{0:T(128)} %widths_ref.1), custom_call_target="tpu_custom_call" | custom-call | tf_op jit(solution)/shard_map/pallas_call | solution.py:402
  43.1 2.1 %copy.11 = bf16[1,32,16,768]{3,2,1,0:T(8,128)(2,1)} copy(bf16[1,32,16,768]{3,2,1,0:T(8,128)(2,1)} %get-tuple-element.8) | data formatting | bytes 1572864
  45.2 1.5 %copy.12 = f32[1,32,16,8]{1,3,2,0:T(8,128)} copy(f32[1,32,16,8]{1,3,2,0:T(8,128)} %bitcast.11) | data formatting | bytes 32768

commit v3 on v2

--- a/solution.py
+++ b/solution.py
@@ -30,30 +30,31 @@
 def dft_table():
     position = np.arange(FINE)
     angles = (position[:, None] * position[None, :] % FINE) * (2.0 * math.pi / FINE)
-    cosine = np.cos(angles) / math.sqrt(FINE)
-    sine = np.sin(angles) / math.sqrt(FINE)
-    table = np.concatenate(
-        [np.concatenate([cosine, -sine], 1), np.concatenate([sine, cosine], 1)], 0
-    ).astype(np.float32)
-    return table
-
-
-def channelize(volt_ref, taps_ref, table, split, table_copy, frames, powers, own):
-    count = volt_ref.shape[0]
+    return (np.stack([np.cos(angles), np.sin(angles)]) / math.sqrt(FINE)).astype(np.float32)
+
+
+def channelize(
+    volt_hbm, taps_ref, volt, volt_copies, table, split, table_copy, start_late, frames, powers, own
+):
+    count = volt_hbm.shape[0]
     frames[count:, :] = jnp.zeros((frames.shape[0] - count, 128), F32)
-    chunk = count // 7
-
-    @pl.loop(0, 7)
-    def _(index):
-        rows = pl.ds(pl.multiple_of(index * chunk, 8), chunk)
-        frames[rows, :] = volt_ref[rows, :].astype(F32)
-
+    for copy, rows in volt_copies:
+        copy.wait()
+        frames[rows, :] = volt[rows, :].astype(F32)
+    table_copy.wait()
+    for index in range(2):
+        exact = table[index]
+        high = exact.astype(BF16)
+        low = (exact - high.astype(F32)).astype(BF16)
+        for which, value in enumerate((high, low)):
+            if index == 0:
+                split[which, 0:FINE, 0:FINE] = value
+                split[which, FINE:, FINE:] = value
+            else:
+                split[which, 0:FINE, FINE:] = -value
+                split[which, FINE:, 0:FINE] = value
+    start_late()
     taps = taps_ref[...]
-    table_copy.wait()
-    table_high = table[...].astype(BF16)
-    table_low = (table[...] - table_high.astype(F32)).astype(BF16)
-    split[0] = table_high
-    split[1] = table_low
 
     def step(index, total):
         start = pl.multiple_of(index * BLOCK, 8)
@@ -93,7 +94,7 @@
 
 def search_kernel(
     beams,
-    volt_ref,
+    volt_hbm,
     taps_ref,
     table_hbm,
     delays_hbm,
@@ -101,6 +102,7 @@
     widths_ref,
     series_ref,
     snr_ref,
+    volt,
     table,
     split,
     delays,
@@ -110,23 +112,32 @@
     slabs,
     total,
     outbox,
+    inbox,
     prefix,
+    best,
     snr_out,
-    snr_in,
     plane_sem,
+    volt_sem,
     load_sem,
     ring_send,
     ring_recv,
     block_send,
     block_recv,
     local_sem,
-    snr_send,
-    snr_recv,
 ):
     me = lax.axis_index("beam")
     sub = lax.axis_index("sub")
     subs = COARSE
     left, right = lax.rem(sub + subs - 1, subs), lax.rem(sub + 1, subs)
+
+    volt_copies = []
+    for half in range(2):
+        rows = pl.ds(half * (volt.shape[0] // 2), volt.shape[0] // 2)
+        copy = pltpu.make_async_copy(volt_hbm.at[rows], volt.at[rows], volt_sem.at[half])
+        copy.start()
+        volt_copies.append((copy, rows))
+    table_copy = pltpu.make_async_copy(table_hbm, table, load_sem.at[0])
+    table_copy.start()
 
     barrier = pltpu.get_barrier_semaphore()
     for side in (left, right):
@@ -155,13 +166,22 @@
     for peer in others_of_place + others_of_plane:
         pl.semaphore_signal(barrier, inc=1, device_id={"beam": peer}, device_id_type=MESH)
 
-    table_copy = pltpu.make_async_copy(table_hbm, table, load_sem.at[0])
-    table_copy.start()
     delays_copy = pltpu.make_async_copy(
         delays_hbm.at[:, pl.ds(pl.multiple_of(sub * 16, 16), 16), :], delays, load_sem.at[1]
     )
-    delays_copy.start()
-    channelize(volt_ref, taps_ref, table, split, table_copy, frames, powers, slabs)
+    channelize(
+        volt_hbm,
+        taps_ref,
+        volt,
+        volt_copies,
+        table,
+        split,
+        table_copy,
+        delays_copy.start,
+        frames,
+        powers,
+        slabs,
+    )
     pl.semaphore_wait(barrier, 2 + planes - 1 + line - 1)
     for peer in others_of_place:
         pl.semaphore_signal(plane_sem, inc=1, device_id={"beam": peer}, device_id_type=MESH)
@@ -210,19 +230,19 @@
             lookup = delays[assign_ref[me, owner], :, lanes]
             lookups[slot, rows, :] = lookup.astype(F32).astype(BF16)
 
-    def product(slot, piece):
-        start = pl.multiple_of(piece * PIECE, PIECE)
-        window = slabs[slot, pl.ds(start, PIECE + SHIFTS), :]
-        shifted = jnp.concatenate(
-            [window[shift : shift + PIECE] for shift in range(SHIFTS)], axis=1
-        )
-        lookup = lookups[slot]
-        onehot = jnp.concatenate(
-            [jnp.where(lookup == BF16(shift), BF16(1), BF16(0)) for shift in range(SHIFTS)],
-            axis=1,
-        )
+    def product(slots, start, count):
+        onehots, shifts = [], []
+        for slot in slots:
+            window = slabs[slot, pl.ds(start, count + SHIFTS), :]
+            lookup = lookups[slot]
+            for shift in range(SHIFTS):
+                shifts.append(window[shift : shift + count])
+                onehots.append(jnp.where(lookup == BF16(shift), BF16(1), BF16(0)))
         return lax.dot_general(
-            onehot, shifted, (((1,), (1,)), ((), ())), preferred_element_type=F32
+            jnp.concatenate(onehots, axis=1),
+            jnp.concatenate(shifts, axis=1),
+            (((1,), (1,)), ((), ())),
+            preferred_element_type=F32,
         )
 
     scale = 1.0 / math.sqrt(COARSE * FINE)
@@ -233,27 +253,27 @@
     def block_copy(piece, owner):
         return pltpu.make_async_remote_copy(
             src_ref=outbox.at[piece, owner],
-            dst_ref=series_ref.at[0, me, :, columns(piece)],
+            dst_ref=inbox.at[piece, me],
             send_sem=block_send.at[piece],
             recv_sem=block_recv.at[piece],
             device_id={"beam": owner},
             device_id_type=MESH,
         )
 
-    def own_copy(piece):
+    def out_copy(piece):
         return pltpu.make_async_copy(
-            outbox.at[piece, me], series_ref.at[0, me, :, columns(piece)], local_sem.at[piece]
+            inbox.at[piece], series_ref.at[0, :, :, columns(piece)], local_sem.at[piece]
         )
 
     def deliver(piece):
         series = (total[piece] * scale).astype(BF16)
         outbox[piece] = series.reshape(beams, 16, PIECE)
-        own_copy(piece).start()
-
         for owner in others:
             block_copy(piece, owner).start()
-
-        count = PIECE + 16
+        inbox[piece, pl.ds(me, 1)] = outbox[piece, pl.ds(me, 1)]
+
+    def add_prefix(piece, series):
+        count = PIECE + MAXW + 16
         triangle = jnp.where(
             lax.broadcasted_iota(jnp.int32, (count, PIECE), 1)
             < lax.broadcasted_iota(jnp.int32, (count, PIECE), 0),
@@ -272,122 +292,130 @@
 
     lane_tiles = beams * 16 // 128
     prefix[:, 0:8, :] = jnp.zeros((lane_tiles, 8, 128), F32)
+    best[...] = jnp.full(best.shape, -jnp.inf, F32)
+    widths = [widths_ref[box] for box in range(NBOX)]
+    own = product((0,), 0, TOUT)
+    for piece in range(PIECES):
+        total[piece] = own[:, piece * PIECE : (piece + 1) * PIECE]
+    pass_on(0)
+    for copy in near[1]:
+        copy.start()
+
     @pl.loop(0, PIECES)
     def _(piece):
-        @pl.when(piece == 2)
-        def _():
-            for copy in near[1]:
-                copy.start()
-
-        total[piece] = product(0, piece)
-
-    pass_on(0)
-
-    @pl.loop(0, 3 * PIECES)
-    def _(step):
-        piece = lax.div(step, 3)
-        slot = 1 + lax.rem(step, 3)
-
-        @pl.when(step == 2)
+        start = pl.multiple_of(piece * PIECE, PIECE)
+        for later in range(1, PIECES):
+
+            @pl.when(piece == later)
+            def _():
+                pass_on(later)
+
+        @pl.loop(1, 3)
+        def _(slot):
+            total[piece] += product((slot,), start, PIECE)
+
+
+        @pl.when(piece == 0)
         def _():
             for copy in near[2]:
                 copy.start()
             pl.semaphore_wait(plane_sem, planes - 1)
 
-        for later in range(1, PIECES):
-
-            @pl.when(step == 3 * later)
-            def _():
-                pass_on(later)
-
         for now in range(PIECES):
 
-            @pl.when(step == 3 * now + 2)
+            @pl.when(piece == now)
             def _():
                 for copy in far[now]:
                     copy.wait_recv()
 
-        total[piece] += product(slot, piece)
-
-        @pl.when(slot == 3)
-        def _():
-            deliver(piece)
-
-    boxcars(widths_ref, prefix, snr_out)
-    snr_in[pl.ds(me, 1)] = snr_out[pl.ds(me, 1)]
-
-    for owner in others:
-        pltpu.make_async_remote_copy(
-            src_ref=snr_out.at[owner],
-            dst_ref=snr_in.at[me],
-            send_sem=snr_send,
-            recv_sem=snr_recv,
-            device_id={"beam": owner},
-            device_id_type=MESH,
-        ).start()
-
-    for piece in range(PIECES):
-        own_copy(piece).wait()
+        total[piece] += product((3,), start, PIECE)
+
+        deliver(piece)
+
+    @pl.loop(0, PIECES)
+    def _(piece):
         all_blocks = pltpu.make_async_remote_copy(
             src_ref=outbox.at[piece, pl.ds(0, beams - 1)],
-            dst_ref=series_ref.at[0, pl.ds(0, beams - 1), :, columns(piece)],
+            dst_ref=inbox.at[piece, pl.ds(0, beams - 1)],
             send_sem=block_send.at[piece],
             recv_sem=block_recv.at[piece],
             device_id={"beam": me},
             device_id_type=MESH,
         )
         all_blocks.wait_recv()
+        out_copy(piece).start()
+        add_prefix(piece, inbox[piece].reshape(beams * 16, PIECE))
+        first = jnp.where(piece == 0, 0, piece * PIECE - MAXW)
+        stop = jnp.where(piece == PIECES - 1, TOUT, (piece + 1) * PIECE - MAXW)
+        boxcars(widths, prefix, best, first, stop)
         all_blocks.wait_send()
-    all_snr = pltpu.make_async_remote_copy(
-        src_ref=snr_out.at[pl.ds(0, beams - 1)],
-        dst_ref=snr_in.at[pl.ds(0, beams - 1)],
-        send_sem=snr_send,
-        recv_sem=snr_recv,
-        device_id={"beam": me},
-        device_id_type=MESH,
-    )
-    all_snr.wait_recv()
-    all_snr.wait_send()
+
+    finish_boxcars(widths, best, snr_out)
+    snr_ref[...] = jnp.transpose(snr_out[:, :, 0:16], (2, 1, 0))
+    for piece in range(PIECES):
+        out_copy(piece).wait()
     for piece in range(PIECES):
         for copy in near[piece] + far[piece]:
             copy.wait_send()
-    snr_ref[...] = jnp.transpose(snr_in[:, :, 0:16], (2, 1, 0))
-
-
-def boxcars(widths_ref, prefix, snr_out):
-    lane_tiles = prefix.shape[0]
-    block = 64
-    widths = [widths_ref[box] for box in range(NBOX)]
-    root = [
-        1.0 / jnp.sqrt(jnp.full((1, 128), width, jnp.int32).astype(F32)) for width in widths
-    ]
-    tail = prefix.shape[1] - TOUT
-    for tile in range(lane_tiles):
-        prefix[tile, TOUT:, :] = jnp.broadcast_to(
-            prefix[tile, TOUT : TOUT + 8, :][0:1], (tail, 128)
-        )
-
-    @pl.loop(0, lane_tiles)
+
+
+def boxcars(widths, prefix, best, first, stop):
+    block = MAXW
+
+    @pl.loop(0, prefix.shape[0])
     def _(tile):
-        def step(index, best):
-            start = pl.multiple_of(index * block, block)
+        def step(index, tops):
+            start = pl.multiple_of(first + index * block, block)
             base = prefix[tile, pl.ds(start, block), :]
             out = []
             for box in range(NBOX):
                 gain = prefix[tile, pl.ds(start + widths[box], block), :] - base
                 top = jnp.max(gain.reshape(block // 8, 8, 128), axis=0)
-                out.append(jnp.maximum(best[box], top))
+                out.append(jnp.maximum(tops[box], top))
             return tuple(out)
 
-        best = lax.fori_loop(
-            0, TOUT // block, step, tuple(jnp.full((8, 128), -jnp.inf, F32) for _ in range(NBOX))
-        )
-        best = jnp.concatenate(
-            [jnp.max(top, axis=0, keepdims=True) * root[box] for box, top in enumerate(best)],
-            axis=0,
-        )
+        tops = tuple(best[tile, box] for box in range(NBOX))
+        tops = lax.fori_loop(0, (stop - first) // block, step, tops)
+        for box in range(NBOX):
+            best[tile, box] = tops[box]
+
+
+def finish_boxcars(widths, best, snr_out):
+    root = [
+        1.0 / jnp.sqrt(jnp.full((1, 128), width, jnp.int32).astype(F32)) for width in widths
+    ]
+
+    @pl.loop(0, best.shape[0])
+    def _(tile):
+        rows = [
+            jnp.max(best[tile, box], axis=0, keepdims=True) * root[box] for box in range(NBOX)
+        ]
+        rows = jnp.concatenate(rows, axis=0)
         for owner in range(8):
-            snr_out[tile * 8 + owner] = pltpu.roll(best, (128 - 16 * owner) % 128, 1)
+            snr_out[tile * 8 + owner] = pltpu.roll(rows, (128 - 16 * owner) % 128, 1)
+
+
+def hand_over(chunks, series_from, snr_from, series_to, snr_to, series, snr, into, out):
+    count = series.shape[1] // chunks
+    steps = [(snr_from, snr, snr_to)]
+    for chunk in range(chunks):
+        rows = pl.ds(chunk * count, count)
+        steps.append((series_from.at[:, rows], series.at[:, rows], series_to.at[:, rows]))
+    loads = [
+        pltpu.make_async_copy(source, held, into.at[index])
+        for index, (source, held, target) in enumerate(steps)
+    ]
+    stores = [
+        pltpu.make_async_copy(held, target, out.at[index])
+        for index, (source, held, target) in enumerate(steps)
+    ]
+    for load in loads:
+        load.start()
+    for load, store in zip(loads, stores):
+        load.wait()
+        store.start()
+    for store in stores:
+        store.wait()
 
 
 def on_device(beams, voltages, pfb_taps, delays, assignment, widths):
@@ -405,10 +433,11 @@
             jax.ShapeDtypeStruct((1, beams, own_span, TOUT), BF16),
             jax.ShapeDtypeStruct((own_span, NBOX, beams), F32),
         ),
-        in_specs=[vmem, vmem, anywhere, anywhere, smem, smem],
+        in_specs=[anywhere, vmem, anywhere, anywhere, smem, smem],
         out_specs=(anywhere, vmem),
         scratch_shapes=[
-            pltpu.VMEM((2 * FINE, 2 * FINE), F32),
+            pltpu.VMEM((4 * voltages.shape[-2], 128), BF16),
+            pltpu.VMEM((2, FINE, FINE), F32),
             pltpu.VMEM((2, 2 * FINE, 2 * FINE), BF16),
             pltpu.VMEM((beams, own_span, chans), jnp.int32),
             pltpu.VMEM((COARSE, rows, FINE), BF16),
@@ -417,18 +446,18 @@
             pltpu.VMEM((COARSE, ROWS, FINE), BF16),
             pltpu.VMEM((PIECES, rows, PIECE), F32),
             pltpu.VMEM((PIECES, beams, own_span, PIECE), BF16),
-            pltpu.VMEM((rows // 128, TOUT + MAXW + 8, 128), F32),
-            pltpu.VMEM((beams, NBOX, 128), F32),
+            pltpu.VMEM((PIECES, beams, own_span, PIECE), BF16),
+            pltpu.VMEM((rows // 128, TOUT + MAXW + 16, 128), F32),
+            pltpu.VMEM((rows // 128, NBOX, 8, 128), F32),
             pltpu.VMEM((beams, NBOX, 128), F32),
             pltpu.SemaphoreType.REGULAR,
+            pltpu.SemaphoreType.DMA((2,)),
             pltpu.SemaphoreType.DMA((2,)),
             pltpu.SemaphoreType.DMA((4 * PIECES,)),
             pltpu.SemaphoreType.DMA((4 * PIECES,)),
             pltpu.SemaphoreType.DMA((PIECES,)),
             pltpu.SemaphoreType.DMA((PIECES,)),
             pltpu.SemaphoreType.DMA((PIECES,)),
-            pltpu.SemaphoreType.DMA,
-            pltpu.SemaphoreType.DMA,
         ],
         compiler_params=pltpu.CompilerParams(
             collective_id=0, has_side_effects=True, vmem_limit_bytes=60 << 20
@@ -441,6 +470,23 @@
         assignment,
         widths,
     )
+    chunks = 8
+    series, snr = pl.pallas_call(
+        functools.partial(hand_over, chunks),
+        out_shape=(
+            jax.ShapeDtypeStruct(series.shape, series.dtype),
+            jax.ShapeDtypeStruct(snr.shape, snr.dtype),
+        ),
+        in_specs=[anywhere, anywhere],
+        out_specs=(anywhere, anywhere),
+        scratch_shapes=[
+            pltpu.VMEM(series.shape, series.dtype),
+            pltpu.VMEM(snr.shape, snr.dtype),
+            pltpu.SemaphoreType.DMA((chunks + 1,)),
+            pltpu.SemaphoreType.DMA((chunks + 1,)),
+        ],
+        compiler_params=pltpu.CompilerParams(vmem_limit_bytes=60 << 20),
+    )(series, snr)
     return series, snr.transpose(2, 0, 1)[None]
 
 

time: 46.9 us -> 45.2 us (0.964)
  local copies, waits for them, and re-layouts: 3.54 us -> 0 us
  Pallas kernels: 42.5 us -> 44.3 us
    unnamed x2 -> x0, local copies, waits for them, and re-layouts: 3.54 us -> none
    pallas_call x0 -> x1, Pallas kernels: none -> 2.03 us  [on_device(): pl.pallas_call(functools.partial(hand_over, chunks), out_shape=(jax.Shape...]
where the time goes in v3:
time: 45.2 us; the launch traced here: 44.9 us
  Pallas kernels  44.3 us (98%)
  between operations  0.64 us (1%)
    pallas_call x1, Pallas kernels, on_device(): pl.pallas_call(functools.partial(search_kernel, beams), out_shape=(jax.Sh...  42.3 us
    pallas_call x1, Pallas kernels, on_device(): pl.pallas_call(functools.partial(hand_over, chunks), out_shape=(jax.Shape...  2.03 us

profile of v3, /device:TPU:1, one launch (start us, length us, event | category | flops | bytes accessed | tf_op | source)
XLA Modules:
  0.0 44.9 jit_solution(16971100858208654271)
XLA Ops:
  0.6 42.3 %shard_map.77 = (bf16[1,32,16,768]{3,2,1,0:T(8,128)(2,1)}, f32[16,8,32]{2,1,0:T(8,128)}) custom-call(bf16[3192,128]{1,0:T(8,128)(2,1)} %bitcast.10, f32[16,256]{1,0:T(8,128)} %taps_ref.1, f32[2,256,256]{2,1,0:T(8,128)} %constant.2.clone.table_hbm, s32[32,64,1024]{2,1,0:T(8,128)} %bitcast.9, s32[32,32]{1,0:T(8,128)} %assign_ref.1, s32[8]{0:T(128)} %widths_ref.1), custom_call_target="tpu_custom_call" | custom-call | tf_op jit(solution)/shard_map/pallas_call | solution.py:430
  42.9 2.0 %shard_map.78 = (bf16[1,32,16,768]{3,2,1,0:T(8,128)(2,1)}, f32[16,8,32]{2,1,0:T(8,128)}) custom-call(bf16[1,32,16,768]{3,2,1,0:T(8,128)(2,1)} %get-tuple-element.6.series_from, f32[16,8,32]{2,1,0:T(8,128)} %get-tuple-element.7.snr_from), custom_call_target="tpu_custom_call" | custom-call | tf_op jit(solution)/shard_map/pallas_call | solution.py:474

commit v4 on v3

--- a/solution.py
+++ b/solution.py
@@ -294,31 +294,35 @@
     prefix[:, 0:8, :] = jnp.zeros((lane_tiles, 8, 128), F32)
     best[...] = jnp.full(best.shape, -jnp.inf, F32)
     widths = [widths_ref[box] for box in range(NBOX)]
-    own = product((0,), 0, TOUT)
-    for piece in range(PIECES):
-        total[piece] = own[:, piece * PIECE : (piece + 1) * PIECE]
-    pass_on(0)
     for copy in near[1]:
         copy.start()
+    @pl.loop(0, PIECES)
+    def _(piece):
+        @pl.when(piece == 2)
+        def _():
+            pass_on(0)
+            for copy in near[2]:
+                copy.start()
+
+        total[piece] = product((0,), pl.multiple_of(piece * PIECE, PIECE), PIECE)
+
 
     @pl.loop(0, PIECES)
     def _(piece):
         start = pl.multiple_of(piece * PIECE, PIECE)
-        for later in range(1, PIECES):
-
-            @pl.when(piece == later)
-            def _():
-                pass_on(later)
-
         @pl.loop(1, 3)
         def _(slot):
             total[piece] += product((slot,), start, PIECE)
 
 
+        for later in range(1, PIECES):
+
+            @pl.when(piece == later - 1)
+            def _():
+                pass_on(later)
+
         @pl.when(piece == 0)
         def _():
-            for copy in near[2]:
-                copy.start()
             pl.semaphore_wait(plane_sem, planes - 1)
 
         for now in range(PIECES):

time: 45.2 us -> 42.6 us (0.942)
  Pallas kernels: 44.3 us -> 41.8 us
    pallas_call x1, Pallas kernels: 42.3 us -> 39.7 us  [on_device(): pl.pallas_call(functools.partial(search_kernel, beams), out_shape=(jax.Sh...]
where the time goes in v4:
time: 42.6 us; the launch traced here: 42.4 us
  Pallas kernels  41.8 us (98%)
  between operations  0.64 us (2%)
    pallas_call x1, Pallas kernels, on_device(): pl.pallas_call(functools.partial(search_kernel, beams), out_shape=(jax.Sh...  39.7 us
    pallas_call x1, Pallas kernels, on_device(): pl.pallas_call(functools.partial(hand_over, chunks), out_shape=(jax.Shape...  2.03 us

profile of v4, /device:TPU:1, one launch (start us, length us, event | category | flops | bytes accessed | tf_op | source)
XLA Modules:
  0.0 42.4 jit_solution(8742050069378999596)
XLA Ops:
  0.6 39.7 %shard_map.77 = (bf16[1,32,16,768]{3,2,1,0:T(8,128)(2,1)}, f32[16,8,32]{2,1,0:T(8,128)}) custom-call(bf16[3192,128]{1,0:T(8,128)(2,1)} %bitcast.10, f32[16,256]{1,0:T(8,128)} %taps_ref.1, f32[2,256,256]{2,1,0:T(8,128)} %constant.2.clone.table_hbm, s32[32,64,1024]{2,1,0:T(8,128)} %bitcast.9, s32[32,32]{1,0:T(8,128)} %assign_ref.1, s32[8]{0:T(128)} %widths_ref.1), custom_call_target="tpu_custom_call" | custom-call | tf_op jit(solution)/shard_map/pallas_call | solution.py:434
  40.4 2.0 %shard_map.78 = (bf16[1,32,16,768]{3,2,1,0:T(8,128)(2,1)}, f32[16,8,32]{2,1,0:T(8,128)}) custom-call(bf16[1,32,16,768]{3,2,1,0:T(8,128)(2,1)} %get-tuple-element.6.series_from, f32[16,8,32]{2,1,0:T(8,128)} %get-tuple-element.7.snr_from), custom_call_target="tpu_custom_call" | custom-call | tf_op jit(solution)/shard_map/pallas_call | solution.py:478

commit v5 on v4

--- a/solution.py
+++ b/solution.py
@@ -21,7 +21,7 @@
 PIECE = 256
 PIECES = TOUT // PIECE
 CUTS = ((0, 272), (272, 256), (528, 256))
-BLOCK = 392
+BLOCK = 784
 MESH = pl.DeviceIdType.MESH
 BF16 = jnp.bfloat16
 F32 = jnp.float32

time: 42.6 us -> 42.1 us (0.988)
  Pallas kernels: 41.8 us -> 41.2 us
    pallas_call x1, Pallas kernels: 39.7 us -> 39.2 us  [on_device(): pl.pallas_call(functools.partial(search_kernel, beams), out_shape=(jax.Sh...]
where the time goes in v5:
time: 42.1 us; the launch traced here: 41.9 us
  Pallas kernels  41.2 us (98%)
  between operations  0.64 us (2%)
    pallas_call x1, Pallas kernels, on_device(): pl.pallas_call(functools.partial(search_kernel, beams), out_shape=(jax.Sh...  39.2 us
    pallas_call x1, Pallas kernels, on_device(): pl.pallas_call(functools.partial(hand_over, chunks), out_shape=(jax.Shape...  2.03 us

profile of v5, /device:TPU:1, one launch (start us, length us, event | category | flops | bytes accessed | tf_op | source)
XLA Modules:
  0.0 41.9 jit_solution(9333027094983570334)
XLA Ops:
  0.6 39.2 %shard_map.77 = (bf16[1,32,16,768]{3,2,1,0:T(8,128)(2,1)}, f32[16,8,32]{2,1,0:T(8,128)}) custom-call(bf16[3192,128]{1,0:T(8,128)(2,1)} %bitcast.10, f32[16,256]{1,0:T(8,128)} %taps_ref.1, f32[2,256,256]{2,1,0:T(8,128)} %constant.2.clone.table_hbm, s32[32,64,1024]{2,1,0:T(8,128)} %bitcast.9, s32[32,32]{1,0:T(8,128)} %assign_ref.1, s32[8]{0:T(128)} %widths_ref.1), custom_call_target="tpu_custom_call" | custom-call | tf_op jit(solution)/shard_map/pallas_call | solution.py:434
  39.9 2.0 %shard_map.78 = (bf16[1,32,16,768]{3,2,1,0:T(8,128)(2,1)}, f32[16,8,32]{2,1,0:T(8,128)}) custom-call(bf16[1,32,16,768]{3,2,1,0:T(8,128)(2,1)} %get-tuple-element.6.series_from, f32[16,8,32]{2,1,0:T(8,128)} %get-tuple-element.7.snr_from), custom_call_target="tpu_custom_call" | custom-call | tf_op jit(solution)/shard_map/pallas_call | solution.py:478

commit v6 on v5

--- a/solution.py
+++ b/solution.py
@@ -34,7 +34,7 @@
 
 
 def channelize(
-    volt_hbm, taps_ref, volt, volt_copies, table, split, table_copy, start_late, frames, powers, own
+    volt_hbm, taps_ref, volt, volt_copies, table, split, table_copy, frames, powers, own
 ):
     count = volt_hbm.shape[0]
     frames[count:, :] = jnp.zeros((frames.shape[0] - count, 128), F32)
@@ -53,7 +53,6 @@
             else:
                 split[which, 0:FINE, FINE:] = -value
                 split[which, FINE:, 0:FINE] = value
-    start_late()
     taps = taps_ref[...]
 
     def step(index, total):
@@ -169,6 +168,7 @@
     delays_copy = pltpu.make_async_copy(
         delays_hbm.at[:, pl.ds(pl.multiple_of(sub * 16, 16), 16), :], delays, load_sem.at[1]
     )
+    delays_copy.start()
     channelize(
         volt_hbm,
         taps_ref,
@@ -177,7 +177,6 @@
         table,
         split,
         table_copy,
-        delays_copy.start,
         frames,
         powers,
         slabs,

time: 42.1 us -> 42.1 us (level)
  no operation moved by 1% of the time
where the time goes in v6:
time: 42.1 us; the launch traced here: 41.9 us
  Pallas kernels  41.2 us (98%)
  between operations  0.64 us (2%)
    pallas_call x1, Pallas kernels, on_device(): pl.pallas_call(functools.partial(search_kernel, beams), out_shape=(jax.Sh...  39.2 us
    pallas_call x1, Pallas kernels, on_device(): pl.pallas_call(functools.partial(hand_over, chunks), out_shape=(jax.Shape...  2.03 us

profile of v6, /device:TPU:1, one launch (start us, length us, event | category | flops | bytes accessed | tf_op | source)
XLA Modules:
  0.0 41.9 jit_solution(1088623318498265053)
XLA Ops:
  0.6 39.2 %shard_map.77 = (bf16[1,32,16,768]{3,2,1,0:T(8,128)(2,1)}, f32[16,8,32]{2,1,0:T(8,128)}) custom-call(bf16[3192,128]{1,0:T(8,128)(2,1)} %bitcast.10, f32[16,256]{1,0:T(8,128)} %taps_ref.1, f32[2,256,256]{2,1,0:T(8,128)} %constant.2.clone.table_hbm, s32[32,64,1024]{2,1,0:T(8,128)} %bitcast.9, s32[32,32]{1,0:T(8,128)} %assign_ref.1, s32[8]{0:T(128)} %widths_ref.1), custom_call_target="tpu_custom_call" | custom-call | tf_op jit(solution)/shard_map/pallas_call | solution.py:433
  39.9 2.0 %shard_map.78 = (bf16[1,32,16,768]{3,2,1,0:T(8,128)(2,1)}, f32[16,8,32]{2,1,0:T(8,128)}) custom-call(bf16[1,32,16,768]{3,2,1,0:T(8,128)(2,1)} %get-tuple-element.6.series_from, f32[16,8,32]{2,1,0:T(8,128)} %get-tuple-element.7.snr_from), custom_call_target="tpu_custom_call" | custom-call | tf_op jit(solution)/shard_map/pallas_call | solution.py:477
